TPU v7x, 32 devices: a whole 2x2x4 slice. The times are simulated.
32 devices in a mesh: ctx: 8 (over y, x, core), seq: 4 (over z).
Axes of the slice: x: 2, y: 2, z: 4, core: 2. Of those that a mesh axis runs over, the one named last changes fastest.
Arguments:
- lin_query: bfloat16 [2048, 4096], P(('seq', 'ctx')), parts along dimension 0, may hold values from -6 to 6
- lin_keys: bfloat16 [2048, 1024], P(('seq', 'ctx')), parts along dimension 0, may hold values from -6 to 6
- lin_values: bfloat16 [2048, 1024], P(('seq', 'ctx')), parts along dimension 0, may hold values from -6 to 6
- state_in: float32 [32, 128, 128], P('seq'), parts along dimension 0, may hold values from -256 to 256
- norm_gain: float32 [4096], replicated, may hold values from 0.1 to 1.9
- soft_query: bfloat16 [2048, 4096], P(('seq', 'ctx')), parts along dimension 0, may hold values from -7 to 7
- soft_keys: bfloat16 [2048, 1024], P(('seq', 'ctx')), parts along dimension 0, may hold values from -7 to 7
- soft_values: bfloat16 [2048, 1024], P(('seq', 'ctx')), parts along dimension 0, may hold values from -6 to 6
Outputs:
- lin_out: bfloat16 [2048, 4096], P(('seq', 'ctx')), parts along dimension 0
- state_out: float32 [32, 128, 128], P('seq'), parts along dimension 0
- soft_out: bfloat16 [2048, 4096], P(('seq', 'ctx')), parts along dimension 0
There are 4 independent parts, one for each index of `seq`. A program takes and returns all parts, laid end to end along the dimension named above; an argument that names none is the same for every part. Nothing has to cross between parts.
All inputs are finite; a program needn't handle non-finite values.
Results may differ from a plain program's by a relative error of at most 0.014.
Values may be sent and summed in bfloat16 or wider, within the bound.
A program may use at most 64 MiB of HBM per device.

v0:
```python
import jax
import jax.numpy as jnp
from jax import lax
from jax.sharding import PartitionSpec as P


def prefix_2(value, axis, join, neutral):
    count, mine = (lax.axis_size(axis), lax.axis_index(axis))
    pieces = lax.all_gather(value, axis)
    so_far = jnp.full_like(value, 0) + jnp.asarray(neutral, value.dtype)

    def step(position, so_far):
        longer = join(so_far, pieces[position])
        return jnp.where(position < mine, longer, so_far)

    return lax.fori_loop(0, count - 1, step, so_far)


def add_states(earlier, later):
    return earlier + later


def linear_blocks(query, keys, values, state):
    total = query.shape[0]
    block = min(512, total)
    steps = total // block
    heads = query.shape[1]
    width = query.shape[2]
    q_blocks = query.reshape(steps, block, heads, width)
    k_blocks = keys.reshape(steps, block, heads, width)
    v_blocks = values.reshape(steps, block, heads, width)
    lower = jnp.tril(jnp.ones((block, block), jnp.float32))

    def advance(memory, pieces):
        q_block, k_block, v_block = pieces
        carried = jnp.einsum(
            "thd,hde->the", q_block.astype(jnp.float32), memory, precision=lax.Precision.HIGHEST
        )
        inner_scores = (
            jnp.einsum("thd,shd->hts", q_block, k_block, preferred_element_type=jnp.float32) * lower
        )
        inner = jnp.einsum(
            "hts,she->the",
            inner_scores,
            v_block.astype(jnp.float32),
            precision=lax.Precision.HIGHEST,
        )
        update = jnp.einsum("thd,the->hde", k_block, v_block, preferred_element_type=jnp.float32)
        return (memory + update, carried + inner)

    final, outputs = lax.scan(advance, state, (q_blocks, k_blocks, v_blocks))
    return (outputs.reshape(total, heads, width), final)


def head_norm(raw, gain):
    square = jnp.mean(raw * raw, axis=-1, keepdims=True)
    return (raw * lax.rsqrt(square + 1e-06) * gain).astype(jnp.bfloat16)


def causal_softmax(pieces):
    query, keys, values = pieces
    total = query.shape[0]
    heads = query.shape[1]
    width = query.shape[2]
    block = min(512, total)
    steps = total // block
    scale = width ** (-0.5)
    q_blocks = query.reshape(steps, block, heads, width)
    key_pos = jnp.arange(total, dtype=jnp.int32)

    def one_block(parts):
        q_block, offset = parts
        scores = (
            jnp.einsum("qmd,kmd->mqk", q_block, keys, preferred_element_type=jnp.float32) * scale
        )
        query_pos = offset + jnp.arange(block, dtype=jnp.int32)
        allowed = key_pos[None, None, :] <= query_pos[None, :, None]
        scores = jnp.where(allowed, scores, -1e30)
        top = jnp.max(scores, axis=-1, keepdims=True)
        expo = jnp.exp(scores - top)
        weights = (expo / jnp.sum(expo, axis=-1, keepdims=True)).astype(jnp.bfloat16)
        return jnp.einsum(
            "mqk,kmd->qmd", weights, values, preferred_element_type=jnp.float32
        ).astype(jnp.bfloat16)

    offsets = jnp.arange(steps, dtype=jnp.int32) * block
    outputs = lax.map(one_block, (q_blocks, offsets))
    return outputs.reshape(total, heads, width)


def shards(
    lin_query, lin_keys, lin_values, state_in, norm_gain, soft_query, soft_keys, soft_values
):
    rows = lin_query.shape[0]
    kv_heads = state_in.shape[0]
    head_dim = state_in.shape[1]
    heads = lin_query.shape[1] // head_dim
    group = heads // kv_heads
    split = (rows, heads, head_dim)
    shared = (rows, kv_heads, head_dim)
    gain = norm_gain.reshape(heads, head_dim)
    query = lin_query.reshape(split)
    keys = lin_keys.reshape(shared)
    values = lin_values.reshape(shared)
    wide_keys = jnp.repeat(keys, group, axis=1)
    wide_values = jnp.repeat(values, group, axis=1)
    local_state = jnp.einsum("thd,the->hde", keys, values, preferred_element_type=jnp.float32)
    prefix = prefix_2(local_state, "ctx", add_states, jnp.zeros_like(local_state))
    before = jnp.repeat(state_in + prefix, group, axis=0)
    raw, ending = linear_blocks(query, wide_keys, wide_values, before)
    lin_out = head_norm(raw, gain).reshape(rows, heads * head_dim)
    state_out = state_in + lax.psum(local_state.astype(jnp.bfloat16), "ctx").astype(jnp.float32)
    soft_input = (soft_query.astype(jnp.float32) + lin_out.astype(jnp.float32)).astype(jnp.bfloat16)
    soft_k = jnp.repeat(soft_keys.reshape(shared), group, axis=1)
    soft_v = jnp.repeat(soft_values.reshape(shared), group, axis=1)
    attended = causal_softmax(
        (
            lax.all_to_all(
                soft_input.reshape(split), "ctx", split_axis=1, concat_axis=0, tiled=True
            ),
            lax.all_to_all(soft_k, "ctx", split_axis=1, concat_axis=0, tiled=True),
            lax.all_to_all(soft_v, "ctx", split_axis=1, concat_axis=0, tiled=True),
        )
    )
    soft_out = lax.all_to_all(attended, "ctx", split_axis=0, concat_axis=1, tiled=True).reshape(
        rows, heads * head_dim
    )
    return (lin_out, state_out, soft_out)


def solution(mesh):
    in_specs = (
        P(("seq", "ctx"), None),
        P(("seq", "ctx"), None),
        P(("seq", "ctx"), None),
        P("seq", None, None),
        P(),
        P(("seq", "ctx"), None),
        P(("seq", "ctx"), None),
        P(("seq", "ctx"), None),
    )
    out_specs = (P(("seq", "ctx"), None), P("seq", None, None), P(("seq", "ctx"), None))
    return jax.shard_map(shards, mesh=mesh, in_specs=in_specs, out_specs=out_specs, check_vma=False)
```

profile of v0, /device:TPU:0, one launch (start us, length us, event | category | flops | bytes accessed | tf_op | source)
XLA Modules:
  0.0 168.5 jit_solution(18187493341674480513)
XLA Ops:
  7.2 2.2 %fusion.21 = (bf16[8,128,128]{2,1,0:T(8,128)(2,1)}, f32[8,128,128]{2,1,0:T(8,128)}) fusion(bf16[64,1024]{1,0:T(8,128)(2,1)} %param.12, bf16[64,1024]{1,0:T(8,128)(2,1)} %param.11), kind=kOutput, calls=%fused_computation.40 | convolution fusion | flops 16908288 | bytes 1048576 | tf_op jit(solution)/shard_map/thd,the->hde/dot_general | solution.py:107
  11.3 5.2 %all-to-all-start.1 = ((bf16[64,32,128]{2,0,1:T(8,128)(2,1)}), bf16[64,32,128]{2,0,1:T(8,128)(2,1)}, u32[]{:S(2)}, u32[]{:S(2)}) async-start(bf16[64,32,128]{2,0,1:T(8,128)(2,1)} %bitcast.10), calls=%async_computation.1 | async-start | bytes 1048576 | tf_op jit(solution)/shard_map/all_to_all | solution.py:121
  18.8 33.4 %all-gather.3.cloned.1.call-done = f32[64,128,128]{2,1,0:T(8,128)} async-done(((f32[8,128,128]{2,1,0:T(8,128)}), f32[64,128,128]{2,1,0:T(8,128)}) %all-gather.3.cloned.1.call-update) | async-done | bytes 4194320 | tf_op jit(solution)/shard_map/all_gather | solution.py:9
  52.2 8.7 %while.9 = (s32[]{:T(128)}, f32[8,128,128]{2,1,0:T(8,128)S(1)}, s32[]{:T(128)}, f32[8,8,128,128]{3,2,1,0:T(8,128)}, s32[]{:T(128)}, /*index=5*/s32[]{:T(128)}) while((s32[]{:T(128)}, f32[8,128,128]{2,1,0:T(8,128)S(1)}, s32[]{:T(128)}, f32[8,8,128,128]{3,2,1,0:T(8,128)}, s32[]{:T(128)}, /*index=5*/s32[]{:T(128)}) %tuple.52), condition=%wide.region_1.2_spmd.clone, body=%wide.region_0.1_spmd.clone.sunk | while | flops 393220 | bytes 1572957 | solution.py:16
  52.2 1.2 add_select_fusion.2
  53.4 1.2 add_select_fusion.2
  54.7 1.2 add_select_fusion.2
  55.9 1.2 add_select_fusion.2
  57.2 1.2 add_select_fusion.2
  58.4 1.2 add_select_fusion.2
  59.7 1.2 add_select_fusion.2
  60.9 48.4 %all-reduce.2.cloned.1.call-done = bf16[8,128,128]{2,1,0:T(8,128)(2,1)} async-done(((bf16[8,128,128]{2,1,0:T(8,128)(2,1)}), bf16[8,128,128]{2,1,0:T(8,128)(2,1)}) %all-reduce.2.cloned.1.call-update) | async-done | bytes 262160 | tf_op jit(solution)/shard_map/psum | solution.py:112
  109.4 1.8 %convert_add_fusion = (f32[8,128,128]{2,1,0:T(8,128)}, f32[8,128,128]{2,1,0:T(8,128)S(1)}) fusion(f32[8,128,128]{2,1,0:T(8,128)S(1)} %copy-done.1, bf16[8,128,128]{2,1,0:T(8,128)(2,1)} %all-reduce.2.cloned.1.call-done, f32[8,128,128]{2,1,0:T(8,128)S(1)} %get-tuple-element.121), kind=kLoop, calls=%fused_computation.26 | loop fusion | flops 393216 | bytes 2359296 | tf_op jit(solution)/shard_map/add | solution.py:112
  111.5 1.1 convolution_bitcast_fusion
  114.6 3.5 %all-to-all-start.2 = ((bf16[64,32,128]{2,0,1:T(8,128)(2,1)}), bf16[64,32,128]{2,0,1:T(8,128)(2,1)S(1)}, u32[]{:S(2)}, u32[]{:S(2)}) async-start(bf16[64,32,128]{2,0,1:T(8,128)(2,1)} %bitcast.14), calls=%async_computation.2 | async-start | bytes 1048576 | tf_op jit(solution)/shard_map/all_to_all | solution.py:122
  118.1 2.2 %fusion.10 = (bf16[8,32,8,128]{3,2,1,0:T(8,128)(2,1)S(1)}, bf16[64,4096]{1,0:T(8,128)(2,1)}) fusion(bf16[64,4096]{1,0:T(8,128)(2,1)} %param.15, f32[64,32,128]{2,0,1:T(8,128)S(1)} %get-tuple-element.152, f32[32,128]{1,0:T(8,128)S(1)} %bitcast.108, f32[64,32]{0,1:T(8,128)S(1)} %add_rsqrt_fusion), kind=kLoop, calls=%fused_computation.21 | loop fusion | flops 1835008 | bytes 2646016
  121.3 6.5 %all-to-all-done.2 = bf16[64,32,128]{2,0,1:T(8,128)(2,1)S(1)} async-done(((bf16[64,32,128]{2,0,1:T(8,128)(2,1)}), bf16[64,32,128]{2,0,1:T(8,128)(2,1)S(1)}, u32[]{:S(2)}, u32[]{:S(2)}) %all-to-all-start.2) | async-done | bytes 524320 | tf_op jit(solution)/shard_map/all_to_all | solution.py:122
  127.8 3.5 %all-to-all-start = ((bf16[64,32,128]{2,0,1:T(8,128)(2,1)}), bf16[64,32,128]{2,0,1:T(8,128)(2,1)S(1)}, u32[]{:S(2)}, u32[]{:S(2)}) async-start(bf16[64,32,128]{2,0,1:T(8,128)(2,1)} %bitcast.95), calls=%async_computation | async-start | bytes 1048576 | tf_op jit(solution)/shard_map/all_to_all | solution.py:118
  131.4 1.1 copy.40
  132.5 8.5 %all-to-all-done = bf16[64,32,128]{2,0,1:T(8,128)(2,1)S(1)} async-done(((bf16[64,32,128]{2,0,1:T(8,128)(2,1)}), bf16[64,32,128]{2,0,1:T(8,128)(2,1)S(1)}, u32[]{:S(2)}, u32[]{:S(2)}) %all-to-all-start) | async-done | bytes 524320 | tf_op jit(solution)/shard_map/all_to_all | solution.py:118
  141.0 3.6 %fusion.22 = (f32[4,512]{1,0:T(4,128)S(1)}, f32[4,512,512]{1,2,0:T(8,128)}) fusion(pred[512,512]{0,1:T(8,128)(4,1)S(1)} %iota_compare_fusion, bf16[512,4,128]{2,0,1:T(8,128)(2,1)S(1)} %bitcast.107, bf16[512,4,128]{2,0,1:T(8,128)(2,1)S(1)} %bitcast.106), kind=kOutput, calls=%fused_computation.41 | convolution fusion | flops 272630272 | bytes 5513216 | tf_op jit(solution)/shard_map/while/body/eval_jaxpr/sub | solution.py:80
  144.6 3.1 %fusion.8 = bf16[512,4,128]{2,0,1:T(8,128)(2,1)S(1)} fusion(bf16[512,4,128]{2,0,1:T(8,128)(2,1)S(1)} %bitcast.105, f32[4,512,512]{1,2,0:T(8,128)} %get-tuple-element.154, f32[4,512]{1,0:T(4,128)S(1)} %get-tuple-element.153), kind=kOutput, calls=%fused_computation.15 | convolution fusion | flops 270794752 | bytes 5251072 | tf_op jit(solution)/shard_map/while/body/eval_jaxpr/mqk,kmd->qmd/dot_general | solution.py:82
  148.1 12.2 %all_to_all.66 = bf16[512,4,128]{2,1,0:T(4,128)(2,1)S(1)} all-to-all(bf16[512,4,128]{2,1,0:T(4,128)(2,1)S(1)} %copy.44), channel_id=1, replica_groups=mesh['ctx'=8,'seq'=4] {'ctx'}, dimensions={0} | all-to-all | bytes 1048576 | tf_op jit(solution)/shard_map/all_to_all | solution.py:125
  160.5 1.2 reshape.96
  (35 shorter events, 8.0 us)
Async XLA Ops:
  7.2 11.2 %copy-start = (bf16[64,4096]{1,0:T(8,128)(2,1)S(1)}, bf16[64,4096]{1,0:T(8,128)(2,1)}, u32[]{:S(2)}) copy-start(bf16[64,4096]{1,0:T(8,128)(2,1)} %param.10) | copy-start | bytes 1572868
  7.2 11.0 %copy-start.2 = (bf16[64,1024]{1,0:T(8,128)(2,1)S(1)}, bf16[64,1024]{1,0:T(8,128)(2,1)}, u32[]{:S(2)}) copy-start(bf16[64,1024]{1,0:T(8,128)(2,1)} %param.12) | copy-start | bytes 393220
  7.2 11.0 %copy-start.3 = (bf16[64,1024]{1,0:T(8,128)(2,1)S(1)}, bf16[64,1024]{1,0:T(8,128)(2,1)}, u32[]{:S(2)}) copy-start(bf16[64,1024]{1,0:T(8,128)(2,1)} %param.17) | copy-start | bytes 393220
  7.2 45.0 %all-gather.3.cloned.1.call-start = ((), (), s32[]{:S(2)}) async-start(), calls=%async_computation.5 | async-start | bytes 4718592 | tf_op jit(solution)/shard_map/all_gather | solution.py:9
  11.3 102.4 %all-to-all-start.1 = ((bf16[64,32,128]{2,0,1:T(8,128)(2,1)}), bf16[64,32,128]{2,0,1:T(8,128)(2,1)}, u32[]{:S(2)}, u32[]{:S(2)}) async-start(bf16[64,32,128]{2,0,1:T(8,128)(2,1)} %bitcast.10), calls=%async_computation.1 | async-start | bytes 1048576 | tf_op jit(solution)/shard_map/all_to_all | solution.py:121
  16.5 92.9 %all-reduce.2.cloned.1.call-start = ((), (), s32[]{:S(2)}) async-start(), calls=%async_computation.4 | async-start | bytes 524288 | tf_op jit(solution)/shard_map/psum | solution.py:112
  18.8 90.6 %copy-start.1 = (f32[8,128,128]{2,1,0:T(8,128)S(1)}, f32[8,128,128]{2,1,0:T(8,128)}, u32[]{:S(2)}) copy-start(f32[8,128,128]{2,1,0:T(8,128)} %param.13) | copy-start | bytes 1572868
  111.5 6.7 %copy-start.4 = (f32[4096]{0:T(1024)S(1)}, f32[4096]{0:T(1024)}, u32[]{:S(2)}) copy-start(f32[4096]{0:T(1024)} %param.14) | copy-start | bytes 49156
  114.6 13.2 %all-to-all-start.2 = ((bf16[64,32,128]{2,0,1:T(8,128)(2,1)}), bf16[64,32,128]{2,0,1:T(8,128)(2,1)S(1)}, u32[]{:S(2)}, u32[]{:S(2)}) async-start(bf16[64,32,128]{2,0,1:T(8,128)(2,1)} %bitcast.14), calls=%async_computation.2 | async-start | bytes 1048576 | tf_op jit(solution)/shard_map/all_to_all | solution.py:122
  127.8 13.2 %all-to-all-start = ((bf16[64,32,128]{2,0,1:T(8,128)(2,1)}), bf16[64,32,128]{2,0,1:T(8,128)(2,1)S(1)}, u32[]{:S(2)}, u32[]{:S(2)}) async-start(bf16[64,32,128]{2,0,1:T(8,128)(2,1)} %bitcast.95), calls=%async_computation | async-start | bytes 1048576 | tf_op jit(solution)/shard_map/all_to_all | solution.py:118
Sparse Core Ops, SparseCore 0:
  10.5 41.6 all-gather.2
  55.8 53.5 all-reduce.1
where the time goes:
time: 169 us; the launch traced here: 168 us
  waiting for transfers between devices  97.5 us (58%)
  between operations  14.3 us (8%)
  other arithmetic  12.7 us (8%)
  starting transfers between devices  12.2 us (7%)
  blocking collectives  12.2 us (7%)
  matrix products  11.4 us (7%)
  local copies, waits for them, and re-layouts  8.07 us (5%)
    psum x1, waiting for transfers between devices, shards(): lax.psum(local_state.astype(jnp.bfloat16), 'ctx').astype(jnp.float32)  48.4 us
    all_gather x1, waiting for transfers between devices, prefix_2(): pieces = lax.all_gather(value, axis)  33.4 us
    all_to_all x1, blocking collectives, shards(): lax.all_to_all(attended, 'ctx', split_axis=0, concat_axis=1, tiled=True)  12.2 us
    select_n x7, other arithmetic, step(): return jnp.where(position < mine, longer, so_far)  8.58 us
    all_to_all x1, waiting for transfers between devices, shards(): lax.all_to_all(soft_input.reshape(split), 'ctx', split_axis=1, concat_axi...  8.46 us
    all_to_all x1, waiting for transfers between devices, shards(): lax.all_to_all(soft_v, 'ctx', split_axis=1, concat_axis=0, tiled=True)  6.53 us
    all_to_all x1, starting transfers between devices, shards(): lax.all_to_all(soft_k, 'ctx', split_axis=1, concat_axis=0, tiled=True)  5.17 us
    sub x1, matrix products, one_block(): expo = jnp.exp(scores - top)  3.6 us
  transfers between devices with their start and end apart: 5, of which 4 were waited for; matrix products, arithmetic and copies ran while one was open for 12% of the time, Pallas kernels for 0%

commit v1 on v0

v1 whole, which is shorter than its diff:
```python
import functools

import jax
import jax.numpy as jnp
from jax import lax
from jax.experimental import pallas as pl
from jax.experimental.pallas import tpu as pltpu
from jax.sharding import PartitionSpec as P

F32 = jnp.float32
BF16 = jnp.bfloat16
LOG2E = 1.4426950408889634


def dot(a, b, dims=((1,), (0,))):
    return lax.dot_general(a, b, (dims, ((), ())), preferred_element_type=F32)


def kernel(
    n, group, width,
    lq_h, lk_h, lv_h, st_h, gain, sq_h, sk_h, sv_h,
    lo_o, st_o, so_o,
    lq, lk, lv, sq, sk, sv, stin, stall, total, raw, qs, ob, out, top, acc,
    loc, pair_s, pair_r, soft_s, soft_r, st_s, st_r, out_s, out_r, out_l,
):
    me = lax.axis_index("ctx")
    c, r = me // 2, me % 2
    sib = 2 * c + 1 - r
    chips = n // 2
    T = lk_h.shape[0]
    T2 = 2 * T
    KW = lk.shape[1]
    QW = lq.shape[1]
    G = KW // width
    R = group * T2

    barrier = pltpu.get_barrier_semaphore()
    for k in range(1, n):
        pl.semaphore_signal(barrier, inc=1, device_id={"ctx": lax.rem(me + k, n)},
                            device_id_type=pl.DeviceIdType.MESH)
    pl.semaphore_wait(barrier, n - 1)

    def rows(d):
        return pl.ds(pl.multiple_of(d * T, T), T)

    def cols(h, w):
        return pl.ds(pl.multiple_of(h * w, w), w)

    def remote(src, dst, ss, rs, dev):
        return pltpu.make_async_remote_copy(
            src_ref=src, dst_ref=dst, send_sem=ss, recv_sem=rs,
            device_id={"ctx": dev}, device_id_type=pl.DeviceIdType.MESH)

    pair = []
    for i, (src, dst, w) in enumerate(((lk_h, lk, KW), (lv_h, lv, KW), (lq_h, lq, QW), (sq_h, sq, QW))):
        cp = remote(src.at[:, cols(1 - r, w)], dst.at[rows(r)], pair_s.at[i], pair_r.at[i], sib)
        cp.start()
        lc = pltpu.make_async_copy(src.at[:, cols(r, w)], dst.at[rows(r)], loc.at[i])
        lc.start()
        rc = remote(src.at[:, cols(r, w)], dst.at[rows(1 - r)], pair_s.at[i], pair_r.at[i], sib)
        pair.append((cp, lc, rc))
    lst = pltpu.make_async_copy(st_h.at[pl.ds(r * G, G)], stin, loc.at[4])
    lst.start()

    softs = ((sk_h, sk), (sv_h, sv))
    own = []
    for a, (src, dst) in enumerate(softs):
        lc = pltpu.make_async_copy(src.at[:, cols(r, KW)], dst.at[rows(me)], loc.at[5 + a])
        lc.start()
        own.append(lc)
        cp = remote(src.at[:, cols(1 - r, KW)], dst.at[rows(me)], soft_s.at[a, sib], soft_r.at[a, me], sib)
        cp.start()

    def soft_send(a, dest, h):
        src, dst = softs[a]
        return remote(src.at[:, h * KW:(h + 1) * KW], dst.at[rows(me)], soft_s.at[a, dest],
                      soft_r.at[a, me], dest)

    def soft_wait(d):
        for a, (src, dst) in enumerate(softs):
            remote(src.at[:, 0:KW], dst.at[rows(d)], soft_s.at[a, d], soft_r.at[a, d], sib).wait_recv()

    for k in range(1, chips):
        @pl.when(c + k < chips)
        def _():
            for h in range(2):
                for a in range(2):
                    soft_send(a, 2 * (c + k) + h, h).start()

    for i in range(2):
        pair[i][1].wait()
        pair[i][2].wait_recv()
    for g in range(G):
        s = slice(g * width, (g + 1) * width)
        stall[c, g] = dot(lk[:, s], lv[:, s], ((0,), (0,))).astype(BF16)

    def state_send(k):
        p = lax.rem(c + k, chips)
        return remote(stall.at[c], stall.at[c], st_s.at[p], st_r.at[c], 2 * p + r)

    def state_recv(k):
        p = lax.rem(c + k, chips)
        return remote(stall.at[p], stall.at[p], st_s.at[p], st_r.at[p], 2 * p + r)

    for k in range(1, chips):
        state_send(k).start()

    for i in range(2, 4):
        pair[i][1].wait()
        pair[i][2].wait_recv()
    tok = lax.rem(lax.broadcasted_iota(jnp.int32, (R, T2), 0), T2)
    keep = lax.broadcasted_iota(jnp.int32, (R, T2), 1) <= tok

    def grouped(ref, g):
        return jnp.concatenate(
            [ref[:, (g * group + i) * width:(g * group + i + 1) * width] for i in range(group)], axis=0)

    for g in range(G):
        s = slice(g * width, (g + 1) * width)
        sc = jnp.where(keep, dot(grouped(lq, g), lk[:, s], ((1,), (1,))), 0.0)
        hi = sc.astype(BF16)
        lo = (sc - hi.astype(F32)).astype(BF16)
        raw[g] = dot(hi, lv[:, s]) + dot(lo, lv[:, s])

    lst.wait()
    for k in range(1, chips):
        state_recv(k).wait_recv()
    for g in range(G):
        before = stin[g]
        whole = before
        for p in range(chips):
            x = stall[p, g].astype(F32)
            whole = whole + x
            before = before + jnp.where(p < c, x, 0.0)
        total[g] = whole
        hi = before.astype(BF16)
        lo = (before - hi.astype(F32)).astype(BF16)
        q = grouped(lq, g)
        full = raw[g] + dot(q, hi) + dot(q, lo)
        inv = lax.rsqrt(jnp.mean(full * full, axis=-1, keepdims=True) + 1e-6)
        full = full * inv
        for i in range(group):
            h = g * group + i
            hs = slice(h * width, (h + 1) * width)
            o = (full[i * T2:(i + 1) * T2] * gain[pl.ds(r * (G * group) + h, 1), :]).astype(BF16)
            ob[:, hs] = o
            qs[g, i * T2:(i + 1) * T2, :] = (sq[:, hs].astype(F32) + o.astype(F32)).astype(BF16)

    def outgo(i, src, dst):
        return (remote(src[1], dst, out_s.at[i], out_r.at[i], sib),
                pltpu.make_async_copy(src[0], dst, out_l.at[i]))

    sends = [
        outgo(0, (ob.at[rows(r)], ob.at[rows(1 - r)]), lo_o.at[:, cols(r, QW)]),
        outgo(1, (total, total), st_o.at[pl.ds(r * G, G)]),
    ]
    for cp, lc in sends:
        cp.start()
        lc.start()

    scale = width ** (-0.5) * LOG2E
    ones = jnp.ones((T2, width), BF16)

    for lc in own:
        lc.wait()
    soft_wait(sib)
    mine = pl.ds(pl.multiple_of(c * T2, T2), T2)
    for g in range(G):
        s = slice(g * width, (g + 1) * width)
        sc = jnp.where(keep, dot(qs[g], sk[mine, s], ((1,), (1,))) * scale, -1e30)
        m = jnp.max(sc, axis=-1, keepdims=True)
        e = jnp.exp2(sc - m).astype(BF16)
        acc[g] = dot(e, jnp.concatenate([sv[mine, s], ones], axis=1))
        top[g] = jnp.broadcast_to(m, (R, width))

    def block(j, _):
        p = c - j
        soft_wait(2 * p)
        soft_wait(2 * p + 1)
        at = pl.ds(pl.multiple_of(p * T2, T2), T2)
        for g in range(G):
            s = slice(g * width, (g + 1) * width)
            sc = dot(qs[g], sk[at, s], ((1,), (1,))) * scale
            old = top[g][:, 0:1]
            m = jnp.maximum(old, jnp.max(sc, axis=-1, keepdims=True))
            e = jnp.exp2(sc - m).astype(BF16)
            acc[g] = acc[g] * jnp.exp2(old - m) + dot(e, jnp.concatenate([sv[at, s], ones], axis=1))
            top[g] = jnp.broadcast_to(m, (R, width))
        return 0

    lax.fori_loop(1, c + 1, block, 0)
    for g in range(G):
        o = (acc[g, :, 0:width] / acc[g, :, width:2 * width]).astype(BF16)
        for i in range(group):
            h = g * group + i
            out[:, h * width:(h + 1) * width] = o[i * T2:(i + 1) * T2]
    sends.append(outgo(2, (out.at[rows(r)], out.at[rows(1 - r)]), so_o.at[:, cols(r, QW)]))
    sends[2][0].start()
    sends[2][1].start()

    for cp, _, _ in pair:
        cp.wait_send()
    for a in range(2):
        soft_send(a, sib, 0).wait_send()
    for k in range(1, chips):
        state_send(k).wait_send()

        @pl.when(c + k < chips)
        def _():
            for h in range(2):
                for a in range(2):
                    soft_send(a, 2 * (c + k) + h, h).wait_send()
    other = 1 - r
    lands = (lo_o.at[:, cols(other, QW)], st_o.at[pl.ds(other * G, G)], so_o.at[:, cols(other, QW)])
    for i, (cp, lc) in enumerate(sends):
        cp.wait_send()
        lc.wait()
        src = (ob.at[rows(r)], total, out.at[rows(r)])[i]
        remote(src, lands[i], out_s.at[i], out_r.at[i], sib).wait_recv()


def shards(n, lin_query, lin_keys, lin_values, state_in, norm_gain, soft_query, soft_keys, soft_values):
    T, D = lin_query.shape
    kvh, width, _ = state_in.shape
    kvd = lin_keys.shape[1]
    heads = D // width
    group = heads // kvh
    G = kvh // 2
    R = group * 2 * T
    chips = n // 2
    hbm = pl.BlockSpec(memory_space=pl.ANY)
    dma = pltpu.SemaphoreType.DMA
    return pl.pallas_call(
        functools.partial(kernel, n, group, width),
        out_shape=(
            jax.ShapeDtypeStruct((T, D), BF16),
            jax.ShapeDtypeStruct(state_in.shape, F32),
            jax.ShapeDtypeStruct((T, D), BF16),
        ),
        in_specs=[hbm, hbm, hbm, hbm, pl.BlockSpec(memory_space=pltpu.VMEM), hbm, hbm, hbm],
        out_specs=(hbm, hbm, hbm),
        scratch_shapes=[
            pltpu.VMEM((2 * T, D // 2), BF16),
            pltpu.VMEM((2 * T, kvd // 2), BF16),
            pltpu.VMEM((2 * T, kvd // 2), BF16),
            pltpu.VMEM((2 * T, D // 2), BF16),
            pltpu.VMEM((n * T, kvd // 2), BF16),
            pltpu.VMEM((n * T, kvd // 2), BF16),
            pltpu.VMEM((G, width, width), F32),
            pltpu.VMEM((chips, G, width, width), BF16),
            pltpu.VMEM((G, width, width), F32),
            pltpu.VMEM((G, R, width), F32),
            pltpu.VMEM((G, R, width), BF16),
            pltpu.VMEM((2 * T, D // 2), BF16),
            pltpu.VMEM((2 * T, D // 2), BF16),
            pltpu.VMEM((G, R, width), F32),
            pltpu.VMEM((G, R, 2 * width), F32),
            dma((7,)), dma((4,)), dma((4,)), dma((2, n)), dma((2, n)),
            dma((chips,)), dma((chips,)), dma((3,)), dma((3,)), dma((3,)),
        ],
        compiler_params=pltpu.CompilerParams(
            collective_id=0, has_side_effects=True, vmem_limit_bytes=48 * 1024 * 1024),
        cost_estimate=pl.CostEstimate(flops=2_000_000_000, bytes_accessed=8_000_000, transcendentals=1_000_000),
    )(lin_query, lin_keys, lin_values, state_in, norm_gain.reshape(heads, width),
      soft_query, soft_keys, soft_values)


def solution(mesh):
    tok = P(("seq", "ctx"), None)
    st = P("seq", None, None)
    return jax.shard_map(
        functools.partial(shards, mesh.shape["ctx"]), mesh=mesh,
        in_specs=(tok, tok, tok, st, P(), tok, tok, tok),
        out_specs=(tok, st, tok), check_vma=False)
```

time: 169 us -> 41.5 us (0.25)
  the two profiles are of different devices: /device:TPU:0 before, /device:TPU:15 now
where the time goes in v1:
time: 41.5 us; the launch traced here: 41.1 us
  Pallas kernels  30.6 us (74%)
  local copies, waits for them, and re-layouts  9.83 us (24%)
  between operations  0.66 us (2%)
    pallas_call x1, Pallas kernels, shards(): pl.pallas_call(functools.partial(kernel, n, group, width), out_shape=(jax...  30.6 us
    unnamed x19, local copies, waits for them, and re-layouts  9.83 us

profile of v1, /device:TPU:15, one launch (start us, length us, event | category | flops | bytes accessed | tf_op | source)
XLA Modules:
  0.0 41.1 jit_solution(13210277423017474519)
XLA Ops:
  0.6 0.0 copy-start
  0.6 1.0 %copy-done = bf16[64,4096]{1,0:T(8,128)(2,1)S(1)} copy-done((bf16[64,4096]{1,0:T(8,128)(2,1)S(1)}, bf16[64,4096]{1,0:T(8,128)(2,1)}, u32[]{:S(2)}) %copy-start) | copy-done | bytes 524312
  1.7 0.0 copy-start.1
  1.7 1.0 %copy-done.1 = f32[8,128,128]{2,1,0:T(8,128)S(1)} copy-done((f32[8,128,128]{2,1,0:T(8,128)S(1)}, f32[8,128,128]{2,1,0:T(8,128)}, u32[]{:S(2)}) %copy-start.1) | copy-done | bytes 524312
  2.7 0.0 copy-start.2
  2.7 1.0 %copy-done.2 = bf16[64,4096]{1,0:T(8,128)(2,1)S(1)} copy-done((bf16[64,4096]{1,0:T(8,128)(2,1)S(1)}, bf16[64,4096]{1,0:T(8,128)(2,1)}, u32[]{:S(2)}) %copy-start.2) | copy-done | bytes 524312
  3.8 0.0 copy-start.3
  3.8 0.9 %copy-done.3 = bf16[64,1024]{1,0:T(8,128)(2,1)S(1)} copy-done((bf16[64,1024]{1,0:T(8,128)(2,1)S(1)}, bf16[64,1024]{1,0:T(8,128)(2,1)}, u32[]{:S(2)}) %copy-start.3) | copy-done | bytes 131096
  4.7 0.0 copy-start.4
  4.7 0.9 %copy-done.4 = bf16[64,1024]{1,0:T(8,128)(2,1)S(1)} copy-done((bf16[64,1024]{1,0:T(8,128)(2,1)S(1)}, bf16[64,1024]{1,0:T(8,128)(2,1)}, u32[]{:S(2)}) %copy-start.4) | copy-done | bytes 131096
  5.6 0.0 copy-start.5
  5.6 0.9 %copy-done.5 = bf16[64,1024]{1,0:T(8,128)(2,1)S(1)} copy-done((bf16[64,1024]{1,0:T(8,128)(2,1)S(1)}, bf16[64,1024]{1,0:T(8,128)(2,1)}, u32[]{:S(2)}) %copy-start.5) | copy-done | bytes 131096
  6.5 0.0 copy-start.6
  6.5 0.9 %copy-done.6 = bf16[64,1024]{1,0:T(8,128)(2,1)S(1)} copy-done((bf16[64,1024]{1,0:T(8,128)(2,1)S(1)}, bf16[64,1024]{1,0:T(8,128)(2,1)}, u32[]{:S(2)}) %copy-start.6) | copy-done | bytes 131096
  7.4 0.0 copy-start.7
  7.4 0.7 %copy-done.7 = f32[4096]{0:T(1024)S(1)} copy-done((f32[4096]{0:T(1024)S(1)}, f32[4096]{0:T(1024)}, u32[]{:S(2)}) %copy-start.7) | copy-done | bytes 16408
  8.1 30.6 %shard_map.103 = (bf16[64,4096]{1,0:T(8,128)(2,1)S(1)}, f32[8,128,128]{2,1,0:T(8,128)S(1)}, bf16[64,4096]{1,0:T(8,128)(2,1)S(1)}) custom-call(bf16[64,4096]{1,0:T(8,128)(2,1)S(1)} %copy-done, bf16[64,1024]{1,0:T(8,128)(2,1)S(1)} %copy-done.3, bf16[64,1024]{1,0:T(8,128)(2,1)S(1)} %copy-done.4, f32[8,128,128]{2,1,0:T(8,128)S(1)} %copy-done.1, ...), custom_call_target="tpu_custom_call" | custom-call | flops 2000000000 | bytes 8000000 | tf_op jit(solution)/shard_map/pallas_call | solution.py:233
  38.7 0.8 %copy.14 = bf16[64,4096]{1,0:T(8,128)(2,1)} copy(bf16[64,4096]{1,0:T(8,128)(2,1)S(1)} %get-tuple-element.6) | data formatting | bytes 1048576
  39.5 0.8 %copy.15 = f32[8,128,128]{2,1,0:T(8,128)} copy(f32[8,128,128]{2,1,0:T(8,128)S(1)} %get-tuple-element.7) | data formatting | bytes 1048576
  40.3 0.8 %copy.16 = bf16[64,4096]{1,0:T(8,128)(2,1)} copy(bf16[64,4096]{1,0:T(8,128)(2,1)S(1)} %get-tuple-element.8) | data formatting | bytes 1048576
Async XLA Ops:
  0.6 1.0 %copy-start = (bf16[64,4096]{1,0:T(8,128)(2,1)S(1)}, bf16[64,4096]{1,0:T(8,128)(2,1)}, u32[]{:S(2)}) copy-start(bf16[64,4096]{1,0:T(8,128)(2,1)} %lq_h.1) | copy-start | bytes 1572868
  1.7 1.0 %copy-start.1 = (f32[8,128,128]{2,1,0:T(8,128)S(1)}, f32[8,128,128]{2,1,0:T(8,128)}, u32[]{:S(2)}) copy-start(f32[8,128,128]{2,1,0:T(8,128)} %st_h.1) | copy-start | bytes 1572868
  2.7 1.0 %copy-start.2 = (bf16[64,4096]{1,0:T(8,128)(2,1)S(1)}, bf16[64,4096]{1,0:T(8,128)(2,1)}, u32[]{:S(2)}) copy-start(bf16[64,4096]{1,0:T(8,128)(2,1)} %sq_h.1) | copy-start | bytes 1572868
  3.8 0.9 %copy-start.3 = (bf16[64,1024]{1,0:T(8,128)(2,1)S(1)}, bf16[64,1024]{1,0:T(8,128)(2,1)}, u32[]{:S(2)}) copy-start(bf16[64,1024]{1,0:T(8,128)(2,1)} %lk_h.1) | copy-start | bytes 393220
  4.7 0.9 %copy-start.4 = (bf16[64,1024]{1,0:T(8,128)(2,1)S(1)}, bf16[64,1024]{1,0:T(8,128)(2,1)}, u32[]{:S(2)}) copy-start(bf16[64,1024]{1,0:T(8,128)(2,1)} %lv_h.1) | copy-start | bytes 393220
  5.6 0.9 %copy-start.5 = (bf16[64,1024]{1,0:T(8,128)(2,1)S(1)}, bf16[64,1024]{1,0:T(8,128)(2,1)}, u32[]{:S(2)}) copy-start(bf16[64,1024]{1,0:T(8,128)(2,1)} %sk_h.1) | copy-start | bytes 393220
  6.5 0.9 %copy-start.6 = (bf16[64,1024]{1,0:T(8,128)(2,1)S(1)}, bf16[64,1024]{1,0:T(8,128)(2,1)}, u32[]{:S(2)}) copy-start(bf16[64,1024]{1,0:T(8,128)(2,1)} %sv_h.1) | copy-start | bytes 393220
  7.4 0.7 %copy-start.7 = (f32[4096]{0:T(1024)S(1)}, f32[4096]{0:T(1024)}, u32[]{:S(2)}) copy-start(f32[4096]{0:T(1024)} %param.12) | copy-start | bytes 49156

commit v2 on v1

--- a/solution.py
+++ b/solution.py
@@ -18,9 +18,9 @@
 
 def kernel(
     n, group, width,
-    lq_h, lk_h, lv_h, st_h, gain, sq_h, sk_h, sv_h,
+    lq_h, lk_h, lv_h, st_h, gain_h, sq_h, sk_h, sv_h,
     lo_o, st_o, so_o,
-    lq, lk, lv, sq, sk, sv, stin, stall, total, raw, qs, ob, out, top, acc,
+    lq, lk, lv, sq, sk, sv, gain, stin, stall, total, raw, qs, ob, out, top, acc,
     loc, pair_s, pair_r, soft_s, soft_r, st_s, st_r, out_s, out_r, out_l,
 ):
     me = lax.axis_index("ctx")
@@ -61,6 +61,8 @@
         pair.append((cp, lc, rc))
     lst = pltpu.make_async_copy(st_h.at[pl.ds(r * G, G)], stin, loc.at[4])
     lst.start()
+    lgain = pltpu.make_async_copy(gain_h, gain, loc.at[7])
+    lgain.start()
 
     softs = ((sk_h, sk), (sv_h, sv))
     own = []
@@ -80,6 +82,23 @@
         for a, (src, dst) in enumerate(softs):
             remote(src.at[:, 0:KW], dst.at[rows(d)], soft_s.at[a, d], soft_r.at[a, d], sib).wait_recv()
 
+    for i in range(2):
+        pair[i][1].wait()
+        pair[i][2].wait_recv()
+    for g in range(G):
+        s = slice(g * width, (g + 1) * width)
+        stall[c, g] = dot(lk[:, s], lv[:, s], ((0,), (0,))).astype(BF16)
+
+    def state_send(k):
+        p = lax.rem(c + k, chips)
+        return remote(stall.at[c], stall.at[c], st_s.at[p], st_r.at[c], 2 * p + r)
+
+    def state_recv(k):
+        p = lax.rem(c + k, chips)
+        return remote(stall.at[p], stall.at[p], st_s.at[p], st_r.at[p], 2 * p + r)
+
+    for k in range(1, chips):
+        state_send(k).start()
     for k in range(1, chips):
         @pl.when(c + k < chips)
         def _():
@@ -87,24 +106,6 @@
                 for a in range(2):
                     soft_send(a, 2 * (c + k) + h, h).start()
 
-    for i in range(2):
-        pair[i][1].wait()
-        pair[i][2].wait_recv()
-    for g in range(G):
-        s = slice(g * width, (g + 1) * width)
-        stall[c, g] = dot(lk[:, s], lv[:, s], ((0,), (0,))).astype(BF16)
-
-    def state_send(k):
-        p = lax.rem(c + k, chips)
-        return remote(stall.at[c], stall.at[c], st_s.at[p], st_r.at[c], 2 * p + r)
-
-    def state_recv(k):
-        p = lax.rem(c + k, chips)
-        return remote(stall.at[p], stall.at[p], st_s.at[p], st_r.at[p], 2 * p + r)
-
-    for k in range(1, chips):
-        state_send(k).start()
-
     for i in range(2, 4):
         pair[i][1].wait()
         pair[i][2].wait_recv()
@@ -123,6 +124,7 @@
         raw[g] = dot(hi, lv[:, s]) + dot(lo, lv[:, s])
 
     lst.wait()
+    lgain.wait()
     for k in range(1, chips):
         state_recv(k).wait_recv()
     for g in range(G):
@@ -219,6 +221,12 @@
         remote(src, lands[i], out_s.at[i], out_r.at[i], sib).wait_recv()
 
 
+def deliver(a, b, c, a_o, b_o, c_o):
+    a_o[...] = a[...]
+    b_o[...] = b[...]
+    c_o[...] = c[...]
+
+
 def shards(n, lin_query, lin_keys, lin_values, state_in, norm_gain, soft_query, soft_keys, soft_values):
     T, D = lin_query.shape
     kvh, width, _ = state_in.shape
@@ -228,17 +236,19 @@
     G = kvh // 2
     R = group * 2 * T
     chips = n // 2
-    hbm = pl.BlockSpec(memory_space=pl.ANY)
+    hbm = pl.BlockSpec(memory_space=pltpu.HBM)
+    near = pl.BlockSpec(memory_space=pl.ANY)
     dma = pltpu.SemaphoreType.DMA
-    return pl.pallas_call(
+    shapes = (
+        jax.ShapeDtypeStruct((T, D), BF16),
+        jax.ShapeDtypeStruct(state_in.shape, F32),
+        jax.ShapeDtypeStruct((T, D), BF16),
+    )
+    results = pl.pallas_call(
         functools.partial(kernel, n, group, width),
-        out_shape=(
-            jax.ShapeDtypeStruct((T, D), BF16),
-            jax.ShapeDtypeStruct(state_in.shape, F32),
-            jax.ShapeDtypeStruct((T, D), BF16),
-        ),
-        in_specs=[hbm, hbm, hbm, hbm, pl.BlockSpec(memory_space=pltpu.VMEM), hbm, hbm, hbm],
-        out_specs=(hbm, hbm, hbm),
+        out_shape=shapes,
+        in_specs=[hbm] * 8,
+        out_specs=(near, near, near),
         scratch_shapes=[
             pltpu.VMEM((2 * T, D // 2), BF16),
             pltpu.VMEM((2 * T, kvd // 2), BF16),
@@ -246,6 +256,7 @@
             pltpu.VMEM((2 * T, D // 2), BF16),
             pltpu.VMEM((n * T, kvd // 2), BF16),
             pltpu.VMEM((n * T, kvd // 2), BF16),
+            pltpu.VMEM((heads, width), F32),
             pltpu.VMEM((G, width, width), F32),
             pltpu.VMEM((chips, G, width, width), BF16),
             pltpu.VMEM((G, width, width), F32),
@@ -255,14 +266,17 @@
             pltpu.VMEM((2 * T, D // 2), BF16),
             pltpu.VMEM((G, R, width), F32),
             pltpu.VMEM((G, R, 2 * width), F32),
-            dma((7,)), dma((4,)), dma((4,)), dma((2, n)), dma((2, n)),
+            dma((8,)), dma((4,)), dma((4,)), dma((2, n)), dma((2, n)),
             dma((chips,)), dma((chips,)), dma((3,)), dma((3,)), dma((3,)),
         ],
         compiler_params=pltpu.CompilerParams(
-            collective_id=0, has_side_effects=True, vmem_limit_bytes=48 * 1024 * 1024),
+            collective_id=0, has_side_effects=True, vmem_limit_bytes=63 * 1024 * 1024),
         cost_estimate=pl.CostEstimate(flops=2_000_000_000, bytes_accessed=8_000_000, transcendentals=1_000_000),
     )(lin_query, lin_keys, lin_values, state_in, norm_gain.reshape(heads, width),
       soft_query, soft_keys, soft_values)
+    return pl.pallas_call(
+        deliver, out_shape=shapes,
+    )(*results)
 
 
 def solution(mesh):

time: 41.5 us -> 29.6 us (0.71)
  local copies, waits for them, and re-layouts: 9.83 us -> 0 us
  Pallas kernels: 30.6 us -> 28.8 us
    unnamed x19 -> x0, local copies, waits for them, and re-layouts: 9.83 us -> none
    pallas_call x1 -> x2, Pallas kernels: 30.6 us -> 28.8 us  [the longest x1 26.3 us: shards(): pl.pallas_call(functools.partial(kernel, n, group, width), out_shape=shap...]
where the time goes in v2:
time: 29.6 us; the launch traced here: 29.5 us
  Pallas kernels  28.8 us (97%)
  between operations  0.64 us (2%)
    pallas_call x1, Pallas kernels, shards(): pl.pallas_call(functools.partial(kernel, n, group, width), out_shape=shap...  26.3 us
    pallas_call x1, Pallas kernels, shards(): return pl.pallas_call(deliver, out_shape=shapes)(*results)  2.53 us

profile of v2, /device:TPU:15, one launch (start us, length us, event | category | flops | bytes accessed | tf_op | source)
XLA Modules:
  0.0 29.5 jit_solution(18441449326959371317)
XLA Ops:
  0.6 26.3 %shard_map.103 = (bf16[64,4096]{1,0:T(8,128)(2,1)}, f32[8,128,128]{2,1,0:T(8,128)}, bf16[64,4096]{1,0:T(8,128)(2,1)}) custom-call(bf16[64,4096]{1,0:T(8,128)(2,1)} %lq_h.1, bf16[64,1024]{1,0:T(8,128)(2,1)} %lk_h.1, bf16[64,1024]{1,0:T(8,128)(2,1)} %lv_h.1, f32[8,128,128]{2,1,0:T(8,128)} %st_h.1, f32[32,128]{1,0:T(8,128)} %bitcast.1, bf16[64,4096]{1,0:T(8,128)(2,1)} %sq_h.1, ...), custom_call_target="tpu_custom_call" | custom-call | flops 2000000000 | bytes 8000000 | tf_op jit(solution)/shard_map/pallas_call | solution.py:247
  26.9 2.5 %shard_map.104 = (bf16[64,4096]{1,0:T(8,128)(2,1)}, f32[8,128,128]{2,1,0:T(8,128)}, bf16[64,4096]{1,0:T(8,128)(2,1)}) custom-call(bf16[64,4096]{1,0:T(8,128)(2,1)} %get-tuple-element.6.a, f32[8,128,128]{2,1,0:T(8,128)} %get-tuple-element.7.b, bf16[64,4096]{1,0:T(8,128)(2,1)} %get-tuple-element.8.c), custom_call_target="tpu_custom_call" | custom-call | tf_op jit(solution)/shard_map/pallas_call | solution.py:277

commit v3 on v2

--- a/solution.py
+++ b/solution.py
@@ -34,42 +34,42 @@
     G = KW // width
     R = group * T2
 
+    def rows(d):
+        return pl.ds(pl.multiple_of(d * T, T), T)
+
+    def cols(h, w):
+        return pl.ds(pl.multiple_of(h * w, w), w)
+
+    def remote(src, dst, ss, rs, dev):
+        return pltpu.make_async_remote_copy(
+            src_ref=src, dst_ref=dst, send_sem=ss, recv_sem=rs,
+            device_id={"ctx": dev}, device_id_type=pl.DeviceIdType.MESH)
+
+    streams = ((lk_h, lk, KW), (lv_h, lv, KW), (lq_h, lq, QW), (sq_h, sq, QW))
+    softs = ((sk_h, sk), (sv_h, sv))
+    near = [pltpu.make_async_copy(src.at[:, cols(r, w)], dst.at[rows(r)], loc.at[i])
+            for i, (src, dst, w) in enumerate(streams)]
+    own = [pltpu.make_async_copy(src.at[:, cols(r, KW)], dst.at[rows(me)], loc.at[5 + a])
+           for a, (src, dst) in enumerate(softs)]
+    lst = pltpu.make_async_copy(st_h.at[pl.ds(r * G, G)], stin, loc.at[4])
+    lgain = pltpu.make_async_copy(gain_h, gain, loc.at[7])
+    for lc in near + own + [lst, lgain]:
+        lc.start()
+
     barrier = pltpu.get_barrier_semaphore()
     for k in range(1, n):
         pl.semaphore_signal(barrier, inc=1, device_id={"ctx": lax.rem(me + k, n)},
                             device_id_type=pl.DeviceIdType.MESH)
     pl.semaphore_wait(barrier, n - 1)
 
-    def rows(d):
-        return pl.ds(pl.multiple_of(d * T, T), T)
-
-    def cols(h, w):
-        return pl.ds(pl.multiple_of(h * w, w), w)
-
-    def remote(src, dst, ss, rs, dev):
-        return pltpu.make_async_remote_copy(
-            src_ref=src, dst_ref=dst, send_sem=ss, recv_sem=rs,
-            device_id={"ctx": dev}, device_id_type=pl.DeviceIdType.MESH)
-
     pair = []
-    for i, (src, dst, w) in enumerate(((lk_h, lk, KW), (lv_h, lv, KW), (lq_h, lq, QW), (sq_h, sq, QW))):
+    for i, (src, dst, w) in enumerate(streams):
         cp = remote(src.at[:, cols(1 - r, w)], dst.at[rows(r)], pair_s.at[i], pair_r.at[i], sib)
         cp.start()
-        lc = pltpu.make_async_copy(src.at[:, cols(r, w)], dst.at[rows(r)], loc.at[i])
-        lc.start()
         rc = remote(src.at[:, cols(r, w)], dst.at[rows(1 - r)], pair_s.at[i], pair_r.at[i], sib)
-        pair.append((cp, lc, rc))
-    lst = pltpu.make_async_copy(st_h.at[pl.ds(r * G, G)], stin, loc.at[4])
-    lst.start()
-    lgain = pltpu.make_async_copy(gain_h, gain, loc.at[7])
-    lgain.start()
-
-    softs = ((sk_h, sk), (sv_h, sv))
-    own = []
+        pair.append((cp, near[i], rc))
+
     for a, (src, dst) in enumerate(softs):
-        lc = pltpu.make_async_copy(src.at[:, cols(r, KW)], dst.at[rows(me)], loc.at[5 + a])
-        lc.start()
-        own.append(lc)
         cp = remote(src.at[:, cols(1 - r, KW)], dst.at[rows(me)], soft_s.at[a, sib], soft_r.at[a, me], sib)
         cp.start()
 
@@ -121,7 +121,7 @@
         sc = jnp.where(keep, dot(grouped(lq, g), lk[:, s], ((1,), (1,))), 0.0)
         hi = sc.astype(BF16)
         lo = (sc - hi.astype(F32)).astype(BF16)
-        raw[g] = dot(hi, lv[:, s]) + dot(lo, lv[:, s])
+        raw[g] = dot(jnp.concatenate([hi, lo], axis=1), jnp.concatenate([lv[:, s], lv[:, s]], axis=0))
 
     lst.wait()
     lgain.wait()
@@ -138,7 +138,7 @@
         hi = before.astype(BF16)
         lo = (before - hi.astype(F32)).astype(BF16)
         q = grouped(lq, g)
-        full = raw[g] + dot(q, hi) + dot(q, lo)
+        full = raw[g] + dot(jnp.concatenate([q, q], axis=1), jnp.concatenate([hi, lo], axis=0))
         inv = lax.rsqrt(jnp.mean(full * full, axis=-1, keepdims=True) + 1e-6)
         full = full * inv
         for i in range(group):
@@ -180,14 +180,17 @@
         soft_wait(2 * p)
         soft_wait(2 * p + 1)
         at = pl.ds(pl.multiple_of(p * T2, T2), T2)
-        for g in range(G):
-            s = slice(g * width, (g + 1) * width)
-            sc = dot(qs[g], sk[at, s], ((1,), (1,))) * scale
-            old = top[g][:, 0:1]
-            m = jnp.maximum(old, jnp.max(sc, axis=-1, keepdims=True))
-            e = jnp.exp2(sc - m).astype(BF16)
-            acc[g] = acc[g] * jnp.exp2(old - m) + dot(e, jnp.concatenate([sv[at, s], ones], axis=1))
-            top[g] = jnp.broadcast_to(m, (R, width))
+        parts = [slice(g * width, (g + 1) * width) for g in range(G)]
+        scs = [dot(qs[g], sk[at, s], ((1,), (1,))) * scale for g, s in enumerate(parts)]
+        olds = [top[g] for g in range(G)]
+        ms = [jnp.maximum(old, jnp.max(sc, axis=-1, keepdims=True)) for old, sc in zip(olds, scs)]
+        es = [jnp.exp2(sc - m[:, 0:1]).astype(BF16)
+              for sc, m in zip(scs, ms)]
+        for g, s in enumerate(parts):
+            new = dot(es[g], jnp.concatenate([sv[at, s], ones], axis=1))
+            fade = jnp.exp2(olds[g] - ms[g])
+            acc[g] = acc[g] * jnp.concatenate([fade, fade], axis=1) + new
+            top[g] = ms[g]
         return 0
 
     lax.fori_loop(1, c + 1, block, 0)

time: 29.6 us -> 28.9 us (0.976)
  Pallas kernels: 28.8 us -> 28.1 us
    pallas_call x1, Pallas kernels: 26.3 us -> 25.6 us  [shards(): pl.pallas_call(functools.partial(kernel, n, group, width), out_shape=shap...]
where the time goes in v3:
time: 28.9 us; the launch traced here: 28.8 us
  Pallas kernels  28.1 us (97%)
  between operations  0.64 us (2%)
    pallas_call x1, Pallas kernels, shards(): pl.pallas_call(functools.partial(kernel, n, group, width), out_shape=shap...  25.6 us
    pallas_call x1, Pallas kernels, shards(): return pl.pallas_call(deliver, out_shape=shapes)(*results)  2.53 us

profile of v3, /device:TPU:15, one launch (start us, length us, event | category | flops | bytes accessed | tf_op | source)
XLA Modules:
  0.0 28.8 jit_solution(9013475015881569176)
XLA Ops:
  0.6 25.6 %shard_map.103 = (bf16[64,4096]{1,0:T(8,128)(2,1)}, f32[8,128,128]{2,1,0:T(8,128)}, bf16[64,4096]{1,0:T(8,128)(2,1)}) custom-call(bf16[64,4096]{1,0:T(8,128)(2,1)} %lq_h.1, bf16[64,1024]{1,0:T(8,128)(2,1)} %lk_h.1, bf16[64,1024]{1,0:T(8,128)(2,1)} %lv_h.1, f32[8,128,128]{2,1,0:T(8,128)} %st_h.1, f32[32,128]{1,0:T(8,128)} %bitcast.1, bf16[64,4096]{1,0:T(8,128)(2,1)} %sq_h.1, ...), custom_call_target="tpu_custom_call" | custom-call | flops 2000000000 | bytes 8000000 | tf_op jit(solution)/shard_map/pallas_call | solution.py:250
  26.2 2.5 %shard_map.104 = (bf16[64,4096]{1,0:T(8,128)(2,1)}, f32[8,128,128]{2,1,0:T(8,128)}, bf16[64,4096]{1,0:T(8,128)(2,1)}) custom-call(bf16[64,4096]{1,0:T(8,128)(2,1)} %get-tuple-element.6.a, f32[8,128,128]{2,1,0:T(8,128)} %get-tuple-element.7.b, bf16[64,4096]{1,0:T(8,128)(2,1)} %get-tuple-element.8.c), custom_call_target="tpu_custom_call" | custom-call | tf_op jit(solution)/shard_map/pallas_call | solution.py:280

commit v4 on v3

--- a/solution.py
+++ b/solution.py
@@ -224,10 +224,18 @@
         remote(src, lands[i], out_s.at[i], out_r.at[i], sib).wait_recv()
 
 
-def deliver(a, b, c, a_o, b_o, c_o):
-    a_o[...] = a[...]
-    b_o[...] = b[...]
-    c_o[...] = c[...]
+def deliver(a, b, c, a_o, b_o, c_o, a_v, b_v, c_v, sem, sem_o):
+    trips = [
+        (pltpu.make_async_copy(x, v, sem.at[i]), pltpu.make_async_copy(v, y, sem_o.at[i]))
+        for i, (x, v, y) in enumerate(((a, a_v, a_o), (b, b_v, b_o), (c, c_v, c_o)))
+    ]
+    for get, _ in trips:
+        get.start()
+    for get, put in trips:
+        get.wait()
+        put.start()
+    for _, put in trips:
+        put.wait()
 
 
 def shards(n, lin_query, lin_keys, lin_values, state_in, norm_gain, soft_query, soft_keys, soft_values):
@@ -278,7 +286,9 @@
     )(lin_query, lin_keys, lin_values, state_in, norm_gain.reshape(heads, width),
       soft_query, soft_keys, soft_values)
     return pl.pallas_call(
-        deliver, out_shape=shapes,
+        deliver, out_shape=shapes, in_specs=[hbm] * 3, out_specs=(hbm,) * 3,
+        scratch_shapes=[pltpu.VMEM(x.shape, x.dtype) for x in shapes] + [dma((3,)), dma((3,))],
+        compiler_params=pltpu.CompilerParams(vmem_limit_bytes=63 * 1024 * 1024),
     )(*results)
 
 

time: 28.9 us -> 28.6 us (0.990)
  Pallas kernels: 28.1 us -> 27.8 us
    pallas_call x1, Pallas kernels: 2.53 us -> 2.23 us  [shards(): pl.pallas_call(deliver, out_shape=shapes, in_specs=[hbm] * 3, out_specs=(...]
where the time goes in v4:
time: 28.6 us; the launch traced here: 28.5 us
  Pallas kernels  27.8 us (97%)
  between operations  0.64 us (2%)
    pallas_call x1, Pallas kernels, shards(): pl.pallas_call(functools.partial(kernel, n, group, width), out_shape=shap...  25.6 us
    pallas_call x1, Pallas kernels, shards(): pl.pallas_call(deliver, out_shape=shapes, in_specs=[hbm] * 3, out_specs=(...  2.23 us

profile of v4, /device:TPU:15, one launch (start us, length us, event | category | flops | bytes accessed | tf_op | source)
XLA Modules:
  0.0 28.5 jit_solution(7124893792401526641)
XLA Ops:
  0.6 25.6 %shard_map.103 = (bf16[64,4096]{1,0:T(8,128)(2,1)}, f32[8,128,128]{2,1,0:T(8,128)}, bf16[64,4096]{1,0:T(8,128)(2,1)}) custom-call(bf16[64,4096]{1,0:T(8,128)(2,1)} %lq_h.1, bf16[64,1024]{1,0:T(8,128)(2,1)} %lk_h.1, bf16[64,1024]{1,0:T(8,128)(2,1)} %lv_h.1, f32[8,128,128]{2,1,0:T(8,128)} %st_h.1, f32[32,128]{1,0:T(8,128)} %bitcast.1, bf16[64,4096]{1,0:T(8,128)(2,1)} %sq_h.1, ...), custom_call_target="tpu_custom_call" | custom-call | flops 2000000000 | bytes 8000000 | tf_op jit(solution)/shard_map/pallas_call | solution.py:258
  26.2 2.2 %shard_map.104 = (bf16[64,4096]{1,0:T(8,128)(2,1)}, f32[8,128,128]{2,1,0:T(8,128)}, bf16[64,4096]{1,0:T(8,128)(2,1)}) custom-call(bf16[64,4096]{1,0:T(8,128)(2,1)} %get-tuple-element.6.a, f32[8,128,128]{2,1,0:T(8,128)} %get-tuple-element.7.b, bf16[64,4096]{1,0:T(8,128)(2,1)} %get-tuple-element.8.c), custom_call_target="tpu_custom_call" | custom-call | tf_op jit(solution)/shard_map/pallas_call | solution.py:288

commit v5 on v4

--- a/solution.py
+++ b/solution.py
@@ -167,13 +167,13 @@
         lc.wait()
     soft_wait(sib)
     mine = pl.ds(pl.multiple_of(c * T2, T2), T2)
-    for g in range(G):
-        s = slice(g * width, (g + 1) * width)
-        sc = jnp.where(keep, dot(qs[g], sk[mine, s], ((1,), (1,))) * scale, -1e30)
-        m = jnp.max(sc, axis=-1, keepdims=True)
-        e = jnp.exp2(sc - m).astype(BF16)
-        acc[g] = dot(e, jnp.concatenate([sv[mine, s], ones], axis=1))
-        top[g] = jnp.broadcast_to(m, (R, width))
+    heads = [slice(g * width, (g + 1) * width) for g in range(G)]
+    first = [jnp.where(keep, dot(qs[g], sk[mine, s], ((1,), (1,))) * scale, -1e30) for g, s in enumerate(heads)]
+    tops = [jnp.max(sc, axis=-1, keepdims=True) for sc in first]
+    exps = [jnp.exp2(sc - m).astype(BF16) for sc, m in zip(first, tops)]
+    for g, s in enumerate(heads):
+        acc[g] = dot(exps[g], jnp.concatenate([sv[mine, s], ones], axis=1))
+        top[g] = jnp.broadcast_to(tops[g], (R, width))
 
     def block(j, _):
         p = c - j

time: 28.6 us -> 28.6 us (level)
  no operation moved by 1% of the time
where the time goes in v5:
time: 28.6 us; the launch traced here: 28.5 us
  Pallas kernels  27.8 us (97%)
  between operations  0.64 us (2%)
    pallas_call x1, Pallas kernels, shards(): pl.pallas_call(functools.partial(kernel, n, group, width), out_shape=shap...  25.6 us
    pallas_call x1, Pallas kernels, shards(): pl.pallas_call(deliver, out_shape=shapes, in_specs=[hbm] * 3, out_specs=(...  2.23 us

profile of v5, /device:TPU:15, one launch (start us, length us, event | category | flops | bytes accessed | tf_op | source)
XLA Modules:
  0.0 28.5 jit_solution(14926213702244255533)
XLA Ops:
  0.6 25.6 %shard_map.103 = (bf16[64,4096]{1,0:T(8,128)(2,1)}, f32[8,128,128]{2,1,0:T(8,128)}, bf16[64,4096]{1,0:T(8,128)(2,1)}) custom-call(bf16[64,4096]{1,0:T(8,128)(2,1)} %lq_h.1, bf16[64,1024]{1,0:T(8,128)(2,1)} %lk_h.1, bf16[64,1024]{1,0:T(8,128)(2,1)} %lv_h.1, f32[8,128,128]{2,1,0:T(8,128)} %st_h.1, f32[32,128]{1,0:T(8,128)} %bitcast.1, bf16[64,4096]{1,0:T(8,128)(2,1)} %sq_h.1, ...), custom_call_target="tpu_custom_call" | custom-call | flops 2000000000 | bytes 8000000 | tf_op jit(solution)/shard_map/pallas_call | solution.py:258
  26.2 2.2 %shard_map.104 = (bf16[64,4096]{1,0:T(8,128)(2,1)}, f32[8,128,128]{2,1,0:T(8,128)}, bf16[64,4096]{1,0:T(8,128)(2,1)}) custom-call(bf16[64,4096]{1,0:T(8,128)(2,1)} %get-tuple-element.6.a, f32[8,128,128]{2,1,0:T(8,128)} %get-tuple-element.7.b, bf16[64,4096]{1,0:T(8,128)(2,1)} %get-tuple-element.8.c), custom_call_target="tpu_custom_call" | custom-call | tf_op jit(solution)/shard_map/pallas_call | solution.py:288
